TPU v7x, 32 devices: a whole 2x2x4 slice. The times are simulated.
32 devices in a mesh: img: 4 (over z), ctx: 2 (over core), tp: 4 (over y, x).
Axes of the slice: x: 2, y: 2, z: 4, core: 2. Of those that a mesh axis runs over, the one named last changes fastest.
Arguments:
- tokens: bfloat16 [8, 24, 24, 768], P('img', 'ctx'), may hold values from -6 to 6
- cotangent: bfloat16 [8, 24, 24, 768], P('img', 'ctx'), may hold values from -6 to 6
- adapter_id: int32 [8], P('img'), may hold values from 0 to 7
- valid_flag: int32 [8], P('img'), may hold values 0 or 1
- regions: int32 [24, 24], P('ctx'), may hold values from 0 to 2
- w_qkv: bfloat16 [768, 3, 768], P('img', None, 'tp'), may hold values from -0.21875 to 0.21875
- b_qkv: bfloat16 [3, 768], P(None, 'tp'), may hold values from -2 to 2
- rel_table: bfloat16 [529, 24], P(None, 'tp'), may hold values from -4 to 4
- w_proj: bfloat16 [768, 768], P('tp', 'img'), may hold values from -0.625 to 0.625
- b_proj: bfloat16 [768], replicated, may hold values from -2 to 2
- w_fc1: bfloat16 [768, 3072], P('img', 'tp'), may hold values from -0.21875 to 0.21875
- b_fc1: bfloat16 [3072], P('tp'), may hold values from -2 to 2
- w_fc2: bfloat16 [3072, 768], P('tp', 'img'), may hold values from -0.109375 to 0.109375
- b_fc2: bfloat16 [768], replicated, may hold values from -2 to 2
- norm_gains: bfloat16 [2, 768], replicated, may hold values from 0.5 to 1.5
- norm_shifts: bfloat16 [2, 768], replicated, may hold values from -2 to 2
- down_main: bfloat16 [8, 3, 12288], P(None, None, ('img', 'ctx')), may hold values from -0.21875 to 0.21875
- down_fc2: bfloat16 [8, 49152], P(None, ('img', 'ctx')), may hold values from -0.109375 to 0.109375
- up_qkv: bfloat16 [8, 36864], P(None, ('img', 'ctx')), may hold values from -1.5 to 1.5
- up_fc1: bfloat16 [8, 49152], P(None, ('img', 'ctx')), may hold values from -1.5 to 1.5
- up_out: bfloat16 [8, 2, 12288], P(None, None, ('img', 'ctx')), may hold values from -1.5 to 1.5
Outputs:
- output: bfloat16 [8, 24, 24, 768], P('img', 'ctx')
- grad_tokens: float32 [8, 24, 24, 768], P('img', 'ctx')
- grad_down_main: float32 [8, 3, 12288], P(None, None, ('img', 'ctx', 'tp'))
- grad_down_fc2: float32 [8, 49152], P(None, ('img', 'ctx', 'tp'))
- grad_up_qkv: float32 [8, 36864], P(None, ('img', 'ctx', 'tp'))
- grad_up_fc1: float32 [8, 49152], P(None, ('img', 'ctx', 'tp'))
- grad_up_out: float32 [8, 2, 12288], P(None, None, ('img', 'ctx', 'tp'))
All inputs are finite; a program needn't handle non-finite values. No bound on the sum of `valid_flag` on one device may be relied on, other than what follows from the above.
Results may differ from a plain program's by a relative error of at most 0.014.
The roundings to bfloat16 on the way count: a program that leaves them out, or rounds other values in their place, can miss the bound.
Values may be sent and summed in bfloat16 or wider, within the bound.
No kernel may reach another device: no remote copies, remote signals or barrier semaphores. Data moves between devices by JAX's collectives and lax.ppermute only.
A program may use at most 256 MiB of HBM per device.

v0:
```python
import jax
import jax.numpy as jnp
from jax import lax
from jax.sharding import PartitionSpec as P

C = 768
HD = 32
FF = 3072
WIN = 12
SHIFT = 6
RANK = 16
ADAPT = 8


epsilon = 1e-05
highest = lax.Precision.HIGHEST


def passed_along(block, axis, distance):
    devices = range(lax.axis_size(axis))
    route = [((i - distance) % len(devices), i) for i in devices]
    return lax.ppermute(block, axis, route)


def contract(pattern, left, right):
    return jnp.einsum(pattern, left, right, preferred_element_type=jnp.float32)


def layer_norm(field, gain, offset):
    average = jnp.mean(field, -1, keepdims=True)
    centred = field - average
    variance = jnp.mean(centred * centred, -1, keepdims=True)
    return centred * lax.rsqrt(variance + epsilon) * gain + offset


def activate(field):
    return jax.nn.gelu(field, approximate=False)


def relative_index():
    offsets_win = jnp.arange(WIN)
    row_diff = offsets_win[:, None, None, None] - offsets_win[None, None, :, None]
    col_diff = offsets_win[None, :, None, None] - offsets_win[None, None, None, :]
    return ((row_diff + WIN - 1) * (2 * WIN - 1) + col_diff + WIN - 1).reshape(WIN * WIN, WIN * WIN)


def to_windows(field):
    images = field.shape[0]
    across = field.shape[2] // WIN
    depth = field.shape[-1]
    field = field.reshape(images, WIN, across, WIN, depth)
    return jnp.transpose(field, (0, 2, 1, 3, 4)).reshape(images, across, WIN * WIN, depth)


def from_windows(field):
    images = field.shape[0]
    across = field.shape[1]
    depth = field.shape[-1]
    field = field.reshape(images, across, WIN, WIN, depth)
    return jnp.transpose(field, (0, 2, 1, 3, 4)).reshape(images, WIN, across * WIN, depth)


def embed_rows(piece_term, size, start, axis_dim):
    dims_list = list(piece_term.shape)
    dims_list[axis_dim] = size
    return lax.dynamic_update_slice_in_dim(
        jnp.zeros(dims_list, jnp.float32), piece_term, start, axis_dim
    )


def per_device(
    tokens,
    cotangent,
    adapter_id,
    valid_flag,
    regions,
    w_qkv,
    b_qkv,
    rel_table,
    w_proj,
    b_proj,
    w_fc1,
    b_fc1,
    w_fc2,
    b_fc2,
    norm_gains,
    norm_shifts,
    down_main,
    down_fc2,
    up_qkv,
    up_fc1,
    up_out,
):
    images = tokens.shape[0]
    height = tokens.shape[1]
    breadth = tokens.shape[2]
    tp_count = lax.axis_size("tp")
    tp_index = lax.axis_index("tp")
    heads_here = rel_table.shape[1]
    local_width = heads_here * HD
    ff_here = w_fc1.shape[1]
    col_width = breadth // tp_count
    col_start = tp_index * col_width
    w_qkv, w_proj, w_fc1, w_fc2 = (
        lax.all_gather(w_qkv, "img", axis=0, tiled=True),
        lax.all_gather(w_proj, "img", axis=1, tiled=True),
        lax.all_gather(w_fc1, "img", axis=0, tiled=True),
        lax.all_gather(w_fc2, "img", axis=1, tiled=True),
    )
    down_main, down_fc2, up_qkv, up_fc1, up_out = (
        lax.all_gather(down_main, ("img", "ctx"), axis=2, tiled=True),
        lax.all_gather(down_fc2, ("img", "ctx"), axis=1, tiled=True),
        lax.all_gather(up_qkv, ("img", "ctx"), axis=1, tiled=True),
        lax.all_gather(up_fc1, ("img", "ctx"), axis=1, tiled=True),
        lax.all_gather(up_out, ("img", "ctx"), axis=2, tiled=True),
    )
    adapter_mask = adapter_id[:, None] == jnp.arange(ADAPT)[None, :]
    adapter_pick = adapter_mask.astype(jnp.bfloat16)
    adapter_hot = adapter_mask.astype(jnp.float32)

    def select_adapter(table):
        return contract("ia,ak->ik", adapter_pick, table.reshape(ADAPT, -1)).astype(jnp.bfloat16)

    main_down = select_adapter(down_main).reshape(images, 3, C, RANK)
    qkv_down = main_down[:, 0]
    proj_down = lax.dynamic_slice_in_dim(main_down[:, 1], tp_index * local_width, local_width, 1)
    fc1_down = main_down[:, 2]
    fc2_down = lax.dynamic_slice_in_dim(
        select_adapter(down_fc2).reshape(images, FF, RANK), tp_index * ff_here, ff_here, 1
    )
    qkv_up = lax.dynamic_slice_in_dim(
        select_adapter(up_qkv).reshape(images, RANK, 3, C), tp_index * local_width, local_width, 3
    )
    fc1_up = lax.dynamic_slice_in_dim(
        select_adapter(up_fc1).reshape(images, RANK, FF), tp_index * ff_here, ff_here, 2
    )
    out_up = select_adapter(up_out).reshape(images, 2, RANK, C)
    proj_up = out_up[:, 0]
    fc2_up = out_up[:, 1]
    rel_bias = jnp.transpose(rel_table.astype(jnp.float32)[relative_index()], (2, 0, 1))
    region_win = to_windows(regions[None, :, :, None])[0, :, :, 0]
    region_mask = jnp.where(region_win[:, :, None] == region_win[:, None, :], 0.0, -100.0).astype(
        jnp.float32
    )
    additive = rel_bias[None, None] + region_mask[None, :, None]
    score_scale = HD ** (-0.5)
    validity = valid_flag.astype(jnp.float32)[:, None, None, None]
    gains = norm_gains.astype(jnp.float32)
    offsets = norm_shifts.astype(jnp.float32)
    inputs = tokens.astype(jnp.float32)

    def first_norm(field):
        return layer_norm(field, gains[0], offsets[0])

    def second_norm(field):
        return layer_norm(field, gains[1], offsets[1])

    def column_share(field):
        return lax.dynamic_slice_in_dim(field, col_start, col_width, 2)

    normed = first_norm(inputs).astype(jnp.bfloat16)
    above_rows = passed_along(normed[:, :SHIFT], "ctx", -1)
    shifted = jnp.roll(jnp.concatenate([normed[:, SHIFT:], above_rows], 1), -SHIFT, 2)
    low_qkv = contract("irjc,icn->irjn", shifted, qkv_down).astype(jnp.bfloat16)
    mixed = (
        contract("irjc,ctd->irjtd", shifted, w_qkv)
        + b_qkv.astype(jnp.float32)
        + contract("irjn,intd->irjtd", low_qkv, qkv_up)
    )
    mixed = mixed.astype(jnp.bfloat16)
    across = breadth // WIN
    mixed_win = to_windows(mixed.reshape(images, height, breadth, 3 * local_width)).reshape(
        images, across, WIN * WIN, 3, heads_here, HD
    )
    queries = mixed_win[:, :, :, 0]
    keys_win = mixed_win[:, :, :, 1]
    values_win = mixed_win[:, :, :, 2]

    def softmax_block():
        scores = score_scale * contract("iwqhd,iwkhd->iwhqk", queries, keys_win) + additive
        return jax.nn.softmax(scores, axis=-1)

    probs_win = softmax_block()
    probs_low = probs_win.astype(jnp.bfloat16)
    attended = contract("iwhqk,iwkhd->iwqhd", probs_low, values_win).astype(jnp.bfloat16)
    attended = jnp.roll(
        from_windows(attended.reshape(images, across, WIN * WIN, local_width)), SHIFT, 2
    )
    below_rows = passed_along(attended[:, height - SHIFT :], "ctx", 1)
    heads_out = jnp.concatenate([below_rows, attended[:, : height - SHIFT]], 1)
    attn_term = contract("irjc,cd->irjd", heads_out, w_proj)
    proj_term = contract("irjc,icn->irjn", heads_out, proj_down)
    attn_total, low_proj = lax.psum((attn_term, proj_term), "tp")
    low_proj = low_proj.astype(jnp.bfloat16)
    residual = inputs + validity * (
        attn_total + b_proj.astype(jnp.float32) + contract("irjn,ind->irjd", low_proj, proj_up)
    )
    normed2 = second_norm(residual).astype(jnp.bfloat16)
    low_proj_cols = column_share(low_proj)
    low_fc1 = contract("irjc,icn->irjn", normed2, fc1_down).astype(jnp.bfloat16)
    preact = (
        contract("irjc,cf->irjf", normed2, w_fc1)
        + b_fc1.astype(jnp.float32)
        + contract("irjn,inf->irjf", low_fc1, fc1_up)
    )
    hidden = activate(preact).astype(jnp.bfloat16)
    mlp_term = contract("irjf,fd->irjd", hidden, w_fc2)
    low_term = contract("irjf,ifn->irjn", hidden, fc2_down)
    mlp_total, low_fc2 = (
        lax.psum(mlp_term.astype(jnp.bfloat16), "tp").astype(jnp.float32),
        lax.psum(low_term.astype(jnp.bfloat16), "tp").astype(jnp.float32),
    )
    low_fc2 = low_fc2.astype(jnp.bfloat16)
    output = (
        residual
        + validity
        * (mlp_total + b_fc2.astype(jnp.float32) + contract("irjn,ind->irjd", low_fc2, fc2_up))
    ).astype(jnp.bfloat16)
    low_fc2_share = column_share(low_fc2)
    grad_output = cotangent.astype(jnp.float32)
    grad_branch = (validity * grad_output).astype(jnp.bfloat16)
    grad_fc2_up = contract("irjn,irjd->ind", low_fc2_share, column_share(grad_branch))
    grad_low_fc2 = contract("irjd,ind->irjn", grad_branch, fc2_up).astype(jnp.bfloat16)
    grad_hidden = contract("irjd,fd->irjf", grad_branch, w_fc2) + contract(
        "irjn,ifn->irjf", grad_low_fc2, fc2_down
    )
    grad_fc2_down = contract("irjf,irjn->ifn", hidden, grad_low_fc2)
    grad_preact = jax.vjp(activate, preact)[1](grad_hidden)[0].astype(jnp.bfloat16)
    grad_fc1_up = contract("irjn,irjf->inf", low_fc1, grad_preact)
    grad_normed2, grad_low_fc1 = lax.psum(
        (
            contract("irjf,cf->irjc", grad_preact, w_fc1),
            contract("irjf,inf->irjn", grad_preact, fc1_up),
        ),
        "tp",
    )
    grad_low_fc1 = grad_low_fc1.astype(jnp.bfloat16)
    grad_normed2 = grad_normed2 + contract("irjn,icn->irjc", grad_low_fc1, fc1_down)
    grad_fc1_down = contract("irjc,irjn->icn", column_share(normed2), column_share(grad_low_fc1))
    grad_residual = grad_output + jax.vjp(second_norm, residual)[1](grad_normed2)[0]
    grad_attn = (validity * grad_residual).astype(jnp.bfloat16)
    grad_proj_up = contract("irjn,irjd->ind", low_proj_cols, column_share(grad_attn))
    grad_low_proj = contract("irjd,ind->irjn", grad_attn, proj_up).astype(jnp.bfloat16)
    grad_heads = (
        contract("irjd,cd->irjc", grad_attn, w_proj)
        + contract("irjn,icn->irjc", grad_low_proj, proj_down)
    ).astype(jnp.bfloat16)
    grad_proj_down = contract("irjc,irjn->icn", heads_out, grad_low_proj)
    above_grad = passed_along(grad_heads[:, :SHIFT], "ctx", -1)
    grad_shift = jnp.roll(jnp.concatenate([grad_heads[:, SHIFT:], above_grad], 1), -SHIFT, 2)
    grad_attended = to_windows(grad_shift).reshape(images, across, WIN * WIN, heads_here, HD)
    probs_win = softmax_block()
    probs_low = probs_win.astype(jnp.bfloat16)
    grad_probs = contract("iwqhd,iwkhd->iwhqk", grad_attended, values_win)
    centre = jnp.sum(grad_probs * probs_win, -1, keepdims=True)
    grad_scores = (probs_win * (grad_probs - centre)).astype(jnp.bfloat16)
    grad_queries = (score_scale * contract("iwhqk,iwkhd->iwqhd", grad_scores, keys_win)).astype(
        jnp.bfloat16
    )
    grad_keys = (score_scale * contract("iwhqk,iwqhd->iwkhd", grad_scores, queries)).astype(
        jnp.bfloat16
    )
    grad_values = contract("iwhqk,iwqhd->iwkhd", probs_low, grad_attended).astype(jnp.bfloat16)
    grad_mixed = jnp.stack([grad_queries, grad_keys, grad_values], 3)
    grad_mixed = from_windows(
        grad_mixed.reshape(images, across, WIN * WIN, 3 * local_width)
    ).reshape(images, height, breadth, 3, local_width)
    grad_qkv_up = contract("irjn,irjtd->intd", low_qkv, grad_mixed)
    grad_shifted, grad_low_qkv = lax.psum(
        (
            contract("irjtd,ctd->irjc", grad_mixed, w_qkv),
            contract("irjtd,intd->irjn", grad_mixed, qkv_up),
        ),
        "tp",
    )
    grad_low_qkv = grad_low_qkv.astype(jnp.bfloat16)
    grad_shifted = grad_shifted + contract("irjn,icn->irjc", grad_low_qkv, qkv_down)
    grad_qkv_down = contract("irjc,irjn->icn", column_share(shifted), column_share(grad_low_qkv))
    grad_shifted = jnp.roll(grad_shifted, SHIFT, 2)
    below_grad = passed_along(
        grad_shifted[:, height - SHIFT :].astype(jnp.bfloat16), "ctx", 1
    ).astype(jnp.float32)
    grad_normed = jnp.concatenate([below_grad, grad_shifted[:, : height - SHIFT]], 1)
    grad_tokens = grad_residual + jax.vjp(first_norm, inputs)[1](grad_normed)[0]

    def by_adapter(term):
        return jnp.einsum("ia,ik->ak", adapter_hot, term.reshape(images, -1), precision=highest)

    term_main = jnp.stack(
        [grad_qkv_down, embed_rows(grad_proj_down, C, tp_index * local_width, 1), grad_fc1_down], 1
    )
    term_fc2 = embed_rows(grad_fc2_down, FF, tp_index * ff_here, 1)
    term_qkv = embed_rows(grad_qkv_up, C, tp_index * local_width, 3)
    term_fc1 = embed_rows(grad_fc1_up, FF, tp_index * ff_here, 2)
    term_out = jnp.stack([grad_proj_up, grad_fc2_up], 1)
    sum_main = by_adapter(term_main).reshape(ADAPT, 3, C * RANK)
    sum_fc2 = by_adapter(term_fc2)
    sum_qkv = by_adapter(term_qkv)
    sum_fc1 = by_adapter(term_fc1)
    sum_out = by_adapter(term_out).reshape(ADAPT, 2, RANK * C)
    grad_main, grad_fc2, grad_qkv, grad_fc1, grad_out = (
        lax.psum_scatter(sum_main, ("img", "ctx", "tp"), scatter_dimension=2, tiled=True),
        lax.psum_scatter(sum_fc2, ("img", "ctx", "tp"), scatter_dimension=1, tiled=True),
        lax.psum_scatter(sum_qkv, ("img", "ctx", "tp"), scatter_dimension=1, tiled=True),
        lax.psum_scatter(sum_fc1, ("img", "ctx", "tp"), scatter_dimension=1, tiled=True),
        lax.psum_scatter(sum_out, ("img", "ctx", "tp"), scatter_dimension=2, tiled=True),
    )
    return (output, grad_tokens, grad_main, grad_fc2, grad_qkv, grad_fc1, grad_out)


def solution(mesh):
    in_specs = (
        P("img", "ctx", None, None),
        P("img", "ctx", None, None),
        P("img"),
        P("img"),
        P("ctx", None),
        P("img", None, "tp"),
        P(None, "tp"),
        P(None, "tp"),
        P("tp", "img"),
        P(),
        P("img", "tp"),
        P("tp"),
        P("tp", "img"),
        P(),
        P(),
        P(),
        P(None, None, ("img", "ctx")),
        P(None, ("img", "ctx")),
        P(None, ("img", "ctx")),
        P(None, ("img", "ctx")),
        P(None, None, ("img", "ctx")),
    )
    out_specs = (
        P("img", "ctx", None, None),
        P("img", "ctx", None, None),
        P(None, None, ("img", "ctx", "tp")),
        P(None, ("img", "ctx", "tp")),
        P(None, ("img", "ctx", "tp")),
        P(None, ("img", "ctx", "tp")),
        P(None, None, ("img", "ctx", "tp")),
    )
    return jax.shard_map(
        per_device, mesh=mesh, in_specs=in_specs, out_specs=out_specs, check_vma=False
    )
```

profile of v0, /device:TPU:0, one launch (start us, length us, event | category | flops | bytes accessed | tf_op | source)
XLA Modules:
  0.0 953.1 jit_solution(10443315287242556696)
XLA Ops:
  16.0 16.3 %all_gather.28 = bf16[8,3,12288]{2,0,1:T(8,128)(2,1)S(1)} all-gather(bf16[8,3,1536]{2,0,1:T(8,128)(2,1)S(1)} %copy-done.71), channel_id=1, replica_groups=mesh['img'=4,'ctx'=2,'tp'=4] {'img','ctx'}, dimensions={2}, use_global_device_ids=true | all-gather | bytes 663552 | tf_op jit(solution)/shard_map/all_gather | solution.py:111
  34.5 15.4 %all_gather.29 = bf16[8,36864]{1,0:T(8,128)(2,1)S(1)} all-gather(bf16[8,4608]{1,0:T(8,128)(2,1)S(1)} %copy-done.72), channel_id=1, replica_groups=mesh['img'=4,'ctx'=2,'tp'=4] {'img','ctx'}, dimensions={1}, use_global_device_ids=true | all-gather | bytes 663552 | tf_op jit(solution)/shard_map/all_gather | solution.py:113
  56.3 39.0 %gather_fusion = f32[20736,6]{1,0:T(8,128)} fusion(f32[529,6]{1,0:T(8,128)S(1)} %copy.105, s32[21504]{0:T(1024)S(1)} %pad_clamp_fusion), kind=kCustom, calls=%fused_computation | custom fusion | bytes 1078272 | tf_op jit(solution)/shard_map/gather | solution.py:140
  95.3 12.2 %copy.106 = f32[6,144,144]{1,2,0:T(8,128)} copy(f32[6,144,144]{0,2,1:T(8,128)} %bitcast.282) | data formatting | bytes 995328 | tf_op jit(solution)/shard_map/transpose | solution.py:140
  110.7 25.1 %all_gather.27 = bf16[768,3,192]{2,0,1:T(8,128)(2,1)S(1)} all-gather(bf16[192,3,192]{2,0,1:T(8,128)(2,1)} %param.26), channel_id=1, replica_groups=mesh['img'=4,'ctx'=2,'tp'=4] {'img'}, dimensions={0}, use_global_device_ids=true | all-gather | bytes 1105920 | tf_op jit(solution)/shard_map/all_gather | solution.py:105
  146.9 4.1 reshape_reshape.19
  169.3 15.1 %all_gather.30 = bf16[192,768]{0,1:T(8,128)(2,1)S(1)} all-gather(bf16[192,192]{0,1:T(8,128)(2,1)S(1)} %copy-done.40), channel_id=1, replica_groups=mesh['img'=4,'ctx'=2,'tp'=4] {'img'}, dimensions={1}, use_global_device_ids=true | all-gather | bytes 368640 | tf_op jit(solution)/shard_map/all_gather | solution.py:106
  189.2 15.8 %all_gather.31 = bf16[8,2,12288]{2,1,0:T(2,128)(2,1)S(1)} all-gather(bf16[8,2,1536]{2,1,0:T(2,128)(2,1)S(1)} %copy-done.79), channel_id=1, replica_groups=mesh['img'=4,'ctx'=2,'tp'=4] {'img','ctx'}, dimensions={2}, use_global_device_ids=true | all-gather | bytes 442368 | tf_op jit(solution)/shard_map/all_gather | solution.py:115
  206.7 21.5 %all_gather.33 = bf16[8,49152]{1,0:T(8,128)(2,1)S(1)} all-gather(bf16[8,6144]{1,0:T(8,128)(2,1)S(1)} %copy-done.65), channel_id=1, replica_groups=mesh['img'=4,'ctx'=2,'tp'=4] {'img','ctx'}, dimensions={1}, use_global_device_ids=true | all-gather | bytes 884736 | tf_op jit(solution)/shard_map/all_gather | solution.py:114
  230.0 18.3 %all_gather.35 = bf16[8,49152]{1,0:T(8,128)(2,1)S(1)} all-gather(bf16[8,6144]{1,0:T(8,128)(2,1)S(1)} %copy-done.66), channel_id=1, replica_groups=mesh['img'=4,'ctx'=2,'tp'=4] {'img','ctx'}, dimensions={1}, use_global_device_ids=true | all-gather | bytes 884736 | tf_op jit(solution)/shard_map/all_gather | solution.py:112
  251.3 19.6 %psum.57 = bf16[2,12,24,16]{2,3,1,0:T(8,128)(2,1)S(1)} all-reduce(f32[2,12,24,16]{2,3,1,0:T(8,128)S(1)} %fusion.76), channel_id=1, replica_groups=mesh['img'=4,'ctx'=2,'tp'=4] {'tp'}, use_global_device_ids=true, to_apply=%region_5.6 | all-reduce | flops 9216 | bytes 55296 | tf_op jit(solution)/shard_map/psum | solution.py:193
  284.5 5.0 multiply_convert_fusion.2
  299.3 21.4 %psum.61 = bf16[2,12,24,16]{2,3,1,0:T(8,128)(2,1)S(1)} all-reduce(f32[2,12,24,16]{2,3,1,0:T(8,128)S(1)} %fusion.87), channel_id=1, replica_groups=mesh['img'=4,'ctx'=2,'tp'=4] {'tp'}, use_global_device_ids=true, to_apply=%region_11.12 | all-reduce | flops 9216 | bytes 55296 | tf_op jit(solution)/shard_map/psum | solution.py:230
  320.7 43.0 %all-reduce.9.cloned.1.call-done = f32[2,12,24,768]{3,2,1,0:T(8,128)} async-done(((f32[2,12,24,768]{3,2,1,0:T(8,128)}), f32[2,12,24,768]{3,2,1,0:T(8,128)}) %all-reduce.9.cloned.1.call-update) | async-done | bytes 1769488 | tf_op jit(solution)/shard_map/psum | solution.py:230
  384.9 5.0 copy.128
  389.9 5.2 reshape_reshape.22
  411.2 19.6 %psum.59 = bf16[2,12,24,16]{2,3,1,0:T(8,128)(2,1)} all-reduce(bf16[2,12,24,16]{2,3,1,0:T(8,128)(2,1)} %convolution_convert_fusion.8), channel_id=1, replica_groups=mesh['img'=4,'ctx'=2,'tp'=4] {'tp'}, use_global_device_ids=true, to_apply=%region_9.10 | all-reduce | flops 9216 | bytes 36864 | tf_op jit(solution)/shard_map/psum | solution.py:211
  454.6 22.2 %psum.63 = bf16[2,12,24,16]{2,3,1,0:T(8,128)(2,1)S(1)} all-reduce(f32[2,12,24,16]{2,3,1,0:T(8,128)S(1)} %convolution_bitcast_fusion.2), channel_id=1, replica_groups=mesh['img'=4,'ctx'=2,'tp'=4] {'tp'}, use_global_device_ids=true, to_apply=%region_16.17 | all-reduce | flops 9216 | bytes 55296 | tf_op jit(solution)/shard_map/psum | solution.py:269
  494.0 33.7 %all-reduce.7.cloned.1.call-done = bf16[2,12,24,768]{3,2,1,0:T(8,128)(2,1)} async-done(((bf16[2,12,24,768]{3,2,1,0:T(8,128)(2,1)}), bf16[2,12,24,768]{3,2,1,0:T(8,128)(2,1)}) %all-reduce.7.cloned.1.call-update) | async-done | bytes 884752 | tf_op jit(solution)/shard_map/psum | solution.py:210
  530.4 6.2 reduce-scatter.14.cloned.1.call-done
  544.4 95.2 %reduce-scatter.8.cloned.1.call-done = f32[8,1536]{1,0:T(8,128)} async-done(((f32[8,49152]{1,0:T(8,128)}), f32[8,1536]{1,0:T(8,128)}) %reduce-scatter.8.cloned.1.call-update) | async-done | bytes 49168 | tf_op jit(solution)/shard_map/reduce_scatter | solution.py:303
  639.5 102.8 %reduce-scatter.12.cloned.1.call-done = f32[8,1536]{1,0:T(8,128)} async-done(((f32[8,49152]{1,0:T(8,128)}), f32[8,1536]{1,0:T(8,128)}) %reduce-scatter.12.cloned.1.call-update) | async-done | bytes 49168 | tf_op jit(solution)/shard_map/reduce_scatter | solution.py:305
  742.4 101.6 %reduce-scatter.6.cloned.1.call-done = f32[8,3,384]{2,0,1:T(8,128)} async-done(((f32[8,3,12288]{2,0,1:T(8,128)}), f32[8,3,384]{2,0,1:T(8,128)}) %reduce-scatter.6.cloned.1.call-update) | async-done | bytes 36880 | tf_op jit(solution)/shard_map/reduce_scatter | solution.py:302
  843.9 101.6 %reduce-scatter.10.cloned.1.call-done = f32[8,1152]{1,0:T(8,128)} async-done(((f32[8,36864]{1,0:T(8,128)}), f32[8,1152]{1,0:T(8,128)}) %reduce-scatter.10.cloned.1.call-update) | async-done | bytes 36880 | tf_op jit(solution)/shard_map/reduce_scatter | solution.py:304
  (368 shorter events, 171.5 us)
Async XLA Ops:
  8.0 264.6 %all-reduce.5.cloned.1.call-start = ((), (), s32[]{:S(2)}) async-start(), calls=%async_computation.5 | async-start | bytes 3538944 | tf_op jit(solution)/shard_map/psum | solution.py:193
  15.5 120.2 %collective-permute-start = (bf16[2,6,24,768]{3,2,1,0:T(8,128)(2,1)}, bf16[2,6,24,768]{3,2,1,0:T(8,128)(2,1)S(1)}, u32[]{:S(2)}, u32[]{:S(2)}) collective-permute-start(bf16[2,6,24,768]{3,2,1,0:T(8,128)(2,1)} %get-tuple-element.44), channel_id=1, source_target_pairs={{4,0},{0,4},{5,1},{1,5},{6,2},{2,6},{7,3},{3,7},{12,8},{8,12},{13,... | collective-permute-start | bytes 1327112 | tf_op jit(solution)/shard_map/ppermute | solution.py:22
  110.7 27.7 %copy-start.54 = (bf16[2,16,3,192]{3,2,1,0:T(4,128)(2,1)}, bf16[2,16,3,192]{3,2,1,0:T(4,128)(2,1)S(1)}, u32[]{:S(2)}) copy-start(bf16[2,16,3,192]{3,2,1,0:T(4,128)(2,1)S(1)} %constant_dynamic-slice_fusion) | copy-start | bytes 110596
  169.2 81.8 %copy-start.24 = (bf16[2,12,18,192]{3,2,1,0:T(8,128)(2,1)}, bf16[2,12,18,192]{3,2,1,0:T(8,128)(2,1)S(1)}, u32[]{:S(2)}) copy-start(bf16[2,12,18,192]{3,2,1,0:T(8,128)(2,1)S(1)} %copy.185) | copy-start | bytes 497668
  169.2 81.7 %copy-start.34 = (bf16[2,12,6,192]{3,2,1,0:T(8,128)(2,1)}, bf16[2,12,6,192]{3,2,1,0:T(8,128)(2,1)S(1)}, u32[]{:S(2)}) copy-start(bf16[2,12,6,192]{3,2,1,0:T(8,128)(2,1)S(1)} %copy.184) | copy-start | bytes 165892
  169.3 15.2 %collective-permute-start.1 = (bf16[2,6,24,192]{3,2,1,0:T(8,128)(2,1)S(1)}, bf16[2,6,24,192]{3,2,1,0:T(8,128)(2,1)S(1)}, u32[]{:S(2)}, u32[]{:S(2)}) collective-permute-start(bf16[2,6,24,192]{3,2,1,0:T(8,128)(2,1)S(1)} %fusion.74), channel_id=1, source_target_pairs={{4,0},{0,4},{5,1},{1,5},{6,2},{2,6},{7,3},{3,7},{12,8},{8,12},{13,... | collective-permute-start | bytes 331784 | tf_op jit(solution)/shard_map/ppermute | solution.py:22
  186.9 92.1 %all-gather.3.cloned.1.call-start = ((), (), s32[]{:S(2)}) async-start(), calls=%async_computation.6 | async-start | bytes 1474560 | tf_op jit(solution)/shard_map/all_gather | solution.py:107
  187.5 102.0 %all-gather.5.cloned.1.call-start = ((), (), s32[]{:S(2)}) async-start(), calls=%async_computation.7 | async-start | bytes 1474560 | tf_op jit(solution)/shard_map/all_gather | solution.py:108
  188.1 175.6 %all-reduce.9.cloned.1.call-start = ((), (), s32[]{:S(2)}) async-start(), calls=%async_computation.9 | async-start | bytes 3538944 | tf_op jit(solution)/shard_map/psum | solution.py:230
  189.1 61.8 %copy-start.36 = (bf16[2,1,768,16]{3,2,1,0:T(8,128)(2,1)}, bf16[2,1,768,16]{3,2,1,0:T(8,128)(2,1)S(1)}, u32[]{:S(2)}) copy-start(bf16[2,1,768,16]{3,2,1,0:T(8,128)(2,1)S(1)} %slice.139) | copy-start | bytes 147460
  204.9 24.4 %copy-start.89 = (bf16[768]{0:T(1024)(128)(2,1)S(1)}, bf16[768]{0:T(1024)(128)(2,1)}, u32[]{:S(2)}) copy-start(bf16[768]{0:T(1024)(128)(2,1)} %param.32) | copy-start | bytes 4612
  204.9 25.0 %copy-start.66 = (bf16[8,6144]{1,0:T(8,128)(2,1)S(1)}, bf16[8,6144]{1,0:T(8,128)(2,1)}, u32[]{:S(2)}) copy-start(bf16[8,6144]{1,0:T(8,128)(2,1)} %param.38) | copy-start | bytes 294916
  205.5 65.4 %copy-start.32 = (bf16[1,2,32,768]{3,2,1,0:T(8,128)(2,1)}, bf16[1,2,32,768]{3,2,1,0:T(8,128)(2,1)S(1)}, u32[]{:S(2)}) copy-start(bf16[1,2,32,768]{3,2,1,0:T(8,128)(2,1)S(1)} %copy.191) | copy-start | bytes 294916
  297.3 190.9 %all-reduce.11.cloned.1.call-start = ((), (), s32[]{:S(2)}) async-start(), calls=%async_computation.10 | async-start | bytes 3538944 | tf_op jit(solution)/shard_map/psum | solution.py:269
  320.7 45.1 %copy-start.42 = (bf16[2,12,24,16]{2,3,1,0:T(8,128)(2,1)}, bf16[2,12,24,16]{2,3,1,0:T(8,128)(2,1)S(1)}, u32[]{:S(2)}) copy-start(bf16[2,12,24,16]{2,3,1,0:T(8,128)(2,1)S(1)} %psum.61) | copy-start | bytes 55300
  370.6 1.4 collective-permute-start.2
  404.3 123.4 %all-reduce.7.cloned.1.call-start = ((), (), s32[]{:S(2)}) async-start(), calls=%async_computation.8 | async-start | bytes 1769472 | tf_op jit(solution)/shard_map/psum | solution.py:210
  408.6 128.1 %reduce-scatter.14.cloned.1.call-start = ((), (), s32[]{:S(2)}) async-start(), calls=%async_computation.15 | async-start | bytes 811008 | tf_op jit(solution)/shard_map/reduce_scatter | solution.py:306
  435.4 204.1 %reduce-scatter.8.cloned.1.call-start = ((), (), s32[]{:S(2)}) async-start(), calls=%async_computation.12 | async-start | bytes 1622016 | tf_op jit(solution)/shard_map/reduce_scatter | solution.py:303
  446.1 296.2 %reduce-scatter.12.cloned.1.call-start = ((), (), s32[]{:S(2)}) async-start(), calls=%async_computation.14 | async-start | bytes 1622016 | tf_op jit(solution)/shard_map/reduce_scatter | solution.py:305
  449.2 394.7 %reduce-scatter.6.cloned.1.call-start = ((), (), s32[]{:S(2)}) async-start(), calls=%async_computation.11 | async-start | bytes 1216512 | tf_op jit(solution)/shard_map/reduce_scatter | solution.py:302
  452.6 25.8 %copy-start.67 = (f32[2,1,768,16]{2,3,0,1:T(8,128)S(1)}, f32[2,1,768,16]{2,3,0,1:T(8,128)}, u32[]{:S(2)}) copy-start(f32[2,1,768,16]{2,3,0,1:T(8,128)} %convolution_bitcast_fusion.7) | copy-start | bytes 294916
  485.3 460.2 %reduce-scatter.10.cloned.1.call-start = ((), (), s32[]{:S(2)}) async-start(), calls=%async_computation.13 | async-start | bytes 1216512 | tf_op jit(solution)/shard_map/reduce_scatter | solution.py:304
  492.1 45.9 %collective-permute-start.3 = (bf16[2,6,24,768]{3,2,1,0:T(8,128)(2,1)}, bf16[2,6,24,768]{3,2,1,0:T(8,128)(2,1)}, u32[]{:S(2)}, u32[]{:S(2)}) collective-permute-start(bf16[2,6,24,768]{3,2,1,0:T(8,128)(2,1)} %fusion.41), channel_id=1, source_target_pairs={{4,0},{0,4},{5,1},{1,5},{6,2},{2,6},{7,3},{3,7},{12,8},{8,12},{13,... | collective-permute-start | bytes 1327112 | tf_op jit(solution)/shard_map/ppermute | solution.py:22
  (84 other events, 401.6 us)
Sparse Core Ops, SparseCore 0:
  187.0 65.8 all-reduce.4
  297.4 66.2 all-reduce.8
  404.4 69.8 all-reduce.10
  477.3 50.3 all-reduce.6
Sparse Core Ops, SparseCore 1:
  188.9 39.4 all-gather.2
  229.8 31.9 all-gather.4
  435.5 101.1 reduce-scatter.13
  543.3 96.1 reduce-scatter.7
  646.2 96.1 reduce-scatter.11
  748.8 95.0 reduce-scatter.5
  850.2 95.2 reduce-scatter.9
where the time goes:
time: 961 us; the launch traced here: 953 us
  waiting for transfers between devices  487 us (51%)
  blocking collectives  210 us (22%)
  local copies, waits for them, and re-layouts  135 us (14%)
  matrix products  70.3 us (7%)
  other arithmetic  32.4 us (3%)
  between operations  17.1 us (2%)
    reduce_scatter x1, waiting for transfers between devices, per_device(): lax.psum_scatter(sum_fc1, ('img', 'ctx', 'tp'), scatter_dimension=1, tile...  103 us
    reduce_scatter x1, waiting for transfers between devices, per_device(): lax.psum_scatter(sum_qkv, ('img', 'ctx', 'tp'), scatter_dimension=1, tile...  102 us
    reduce_scatter x1, waiting for transfers between devices, per_device(): lax.psum_scatter(sum_main, ('img', 'ctx', 'tp'), scatter_dimension=2, til...  102 us
    reduce_scatter x1, waiting for transfers between devices, per_device(): lax.psum_scatter(sum_fc2, ('img', 'ctx', 'tp'), scatter_dimension=1, tile...  95.2 us
    dot_general x43, matrix products, contract(): return jnp.einsum(pattern, left, right, preferred_element_type=jnp.float32)  60.5 us
    psum x1, waiting for transfers between devices, per_device(): lax.psum((contract('irjf,cf->irjc', grad_preact, w_fc1), contract('irjf,i...  43 us
    gather x1, local copies, waits for them, and re-layouts, per_device(): rel_table.astype(jnp.float32)[relative_index()]  39 us
    psum x1, waiting for transfers between devices, per_device(): lax.psum(mlp_term.astype(jnp.bfloat16), 'tp').astype(jnp.float32)  33.7 us
  transfers between devices with their start and end apart: 15, of which 8 were waited for; matrix products, arithmetic and copies ran while one was open for 15% of the time, Pallas kernels for 0%

commit v1 on v0

v1 whole, which is shorter than its diff:
```python
import jax
import jax.numpy as jnp
from jax import lax
from jax.sharding import PartitionSpec as P

C = 768
HD = 32
FF = 3072
WIN = 12
SHIFT = 6
RANK = 16
ADAPT = 8
RELS = 529
TOK = WIN * WIN
SCALE = HD ** (-0.5)
EPS = 1e-05

bf16 = jnp.bfloat16
f32 = jnp.float32


def dot(left, right):
    return jnp.dot(left, right, preferred_element_type=f32)


def dot_t(left, right):
    return lax.dot_general(left, right, (((1,), (1,)), ((), ())), preferred_element_type=f32)


def tdot(left, right):
    return lax.dot_general(left, right, (((0,), (0,)), ((), ())), preferred_element_type=f32)


def swap_ctx(v):
    return lax.ppermute(v, "ctx", [(0, 1), (1, 0)])


def swap_x(v):
    return lax.ppermute(v, "tp", [(0, 1), (1, 0), (2, 3), (3, 2)])


def swap_y(v):
    return lax.ppermute(v, "tp", [(0, 2), (2, 0), (1, 3), (3, 1)])


def ring(v):
    count = lax.axis_size("img")
    if count > 8:
        whole = lax.all_gather(v, "img", axis=0)
        here = lax.axis_index("img")
        return [lax.dynamic_index_in_dim(whole, (here - k) % count, 0, False) for k in range(count)]
    held = [v]
    for _ in range(count - 1):
        held.append(lax.ppermute(held[-1], "img", [(i, (i + 1) % count) for i in range(count)]))
    return held


def spread_first(v):
    held = ring(v)
    half = len(held) // 2
    by_x = [swap_x(a) for a in held]
    by_y = [swap_y(a) for a in held]
    by_xy = [swap_y(a) for a in by_x[:half]] + [swap_x(a) for a in by_y[half:]]
    out = {}
    for k in range(len(held)):
        out[k, 0], out[k, 1], out[k, 2], out[k, 3] = held[k], by_x[k], by_y[k], by_xy[k]
    return out


def spread_last(v, first, second, one, two):
    held = ring(jnp.stack([v, first(v)]))
    out = {}
    for k, pair in enumerate(held):
        other = second(pair)
        out[k, 0], out[k, one] = pair[0], pair[1]
        out[k, two], out[k, one + two] = other[0], other[1]
    return out


def assemble(pieces, z, c, t):
    count = lax.axis_size("img")
    rows, cols = pieces[0, 0].shape
    whole = jnp.zeros((count * 2 * rows, 4 * cols), bf16)
    for (k, j), piece in pieces.items():
        other = swap_ctx(piece)
        top = ((z - k) % count) * 2 * rows
        left = (t ^ j) * cols
        whole = lax.dynamic_update_slice(whole, piece, (top + c * rows, left))
        whole = lax.dynamic_update_slice(whole, other, (top + (1 - c) * rows, left))
    return whole


def norm_parts(field):
    average = jnp.mean(field, -1, keepdims=True)
    centred = field - average
    variance = jnp.mean(centred * centred, -1, keepdims=True)
    scale = lax.rsqrt(variance + EPS)
    return centred * scale, scale


def norm_back(grad, gain, unit, scale):
    scaled = grad * gain
    return scale * (
        scaled
        - jnp.mean(scaled, -1, keepdims=True)
        - unit * jnp.mean(scaled * unit, -1, keepdims=True)
    )


def bias_of(table):
    heads = table.shape[0]
    span = 2 * WIN - 1
    q_col = jnp.arange(WIN)[:, None, None]
    step = jnp.arange(span)[None, :, None]
    k_col = jnp.arange(WIN)[None, None, :]
    index = ((span - 1 - step) * span + q_col - k_col + WIN - 1).reshape(-1)
    chosen = (jnp.arange(RELS)[:, None] == index[None, :]).astype(bf16)
    strips = dot(table, chosen).reshape(heads, WIN, span * WIN)
    rows = [strips[:, :, (WIN - 1 - r) * WIN :][:, :, :TOK] for r in range(WIN)]
    return jnp.stack(rows, 1).reshape(heads, TOK, TOK)


def per_device(
    tokens,
    cotangent,
    adapter_id,
    valid_flag,
    regions,
    w_qkv,
    b_qkv,
    rel_table,
    w_proj,
    b_proj,
    w_fc1,
    b_fc1,
    w_fc2,
    b_fc2,
    norm_gains,
    norm_shifts,
    down_main,
    down_fc2,
    up_qkv,
    up_fc1,
    up_out,
):
    z, c, t = (lax.axis_index(name) for name in ("img", "ctx", "tp"))
    z_count, t_count = lax.axis_size("img"), lax.axis_size("tp")
    images, height, breadth = tokens.shape[:3]
    across = breadth // WIN
    image, column = t // across, t % across
    heads_here = rel_table.shape[1]
    heads = heads_here * t_count
    wide = heads_here * HD
    ff_here = w_fc1.shape[1]

    both = jnp.stack([lax.dynamic_index_in_dim(a, image, 0, False) for a in (tokens, cotangent)])
    both = lax.dynamic_slice_in_dim(jnp.roll(both, -SHIFT, 2), column * WIN, WIN, 2)
    upper = swap_ctx(both[:, :SHIFT])
    inputs, grad_output = jnp.concatenate([both[:, SHIFT:], upper], 1).reshape(2, TOK, C).astype(f32)

    def half(v):
        rows = v.shape[0] // 2
        return lax.dynamic_slice_in_dim(v, c * rows, rows, 0)

    group_a = jnp.concatenate([half(w_qkv).reshape(-1, 3 * wide), half(w_proj.T)], 1)
    group_b = half(w_fc1)
    group_c = half(w_fc2.T)
    full_a = assemble(spread_first(group_a), z, c, t).reshape(C, t_count, 4 * wide)
    full_fc1 = assemble(spread_last(group_b, swap_x, swap_y, 1, 2), z, c, t)
    full_fc2 = assemble(spread_last(group_c, swap_y, swap_x, 2, 1), z, c, t)
    full_qkv = full_a[:, :, : 3 * wide].reshape(C, 3 * C)
    full_proj = full_a[:, :, 3 * wide :].reshape(C, C)

    ids = lax.all_gather(adapter_id, "img")
    tables = jnp.concatenate(
        [v.reshape(ADAPT, -1) for v in (down_main, down_fc2, up_qkv, up_fc1, up_out)], 1
    )
    wanted = lax.dynamic_index_in_dim(ids, image, 1, False)
    pick = (wanted[:, None] == jnp.arange(ADAPT)[None, :]).astype(bf16)
    sent = dot(pick, tables).astype(bf16)
    mine = lax.all_to_all(sent, "img", 0, 0, tiled=True)
    theirs = swap_ctx(mine)
    mine, theirs = jnp.where(c == 0, mine, theirs), jnp.where(c == 0, theirs, mine)
    owned = jnp.stack([mine, theirs], 1).reshape(2 * z_count, -1)
    sizes = [v.size // ADAPT for v in (down_main, down_fc2, up_qkv, up_fc1, up_out)]
    cuts = [sum(sizes[:i]) for i in range(6)]
    main, fc2, qkv, fc1, out = (owned[:, cuts[i] : cuts[i + 1]] for i in range(5))
    main = main.reshape(2 * z_count, 3, -1).transpose(1, 0, 2).reshape(3, C, RANK)
    out = out.reshape(2 * z_count, 2, -1).transpose(1, 0, 2).reshape(2, RANK, C)
    qkv_down, proj_down, fc1_down = main
    fc2_down = fc2.reshape(FF, RANK)
    qkv_up = qkv.reshape(RANK, 3, t_count, wide).transpose(0, 2, 1, 3).reshape(RANK, 3 * C)
    fc1_up = fc1.reshape(RANK, FF)
    proj_up, fc2_up = out

    small = jnp.concatenate([b_qkv.reshape(-1), b_fc1, rel_table.T.reshape(-1)])
    small = lax.all_gather(small, "tp")
    bias_qkv = small[:, : 3 * wide].reshape(-1).astype(f32)
    bias_fc1 = small[:, 3 * wide : 3 * wide + ff_here].reshape(-1).astype(f32)
    table = small[:, 3 * wide + ff_here :].reshape(heads, RELS)

    region = lax.dynamic_slice_in_dim(regions, column * WIN, WIN, 1).reshape(TOK)
    mask = jnp.where(region[:, None] == region[None, :], 0.0, -100.0).astype(f32)
    additive = bias_of(table) + mask[None]
    valid = lax.dynamic_index_in_dim(valid_flag, image, 0, False).astype(f32)
    gains = norm_gains.astype(f32)
    shifts = norm_shifts.astype(f32)

    unit1, scale1 = norm_parts(inputs)
    shifted = (unit1 * gains[0] + shifts[0]).astype(bf16)
    low_qkv = dot(shifted, qkv_down).astype(bf16)
    mixed = (dot(shifted, full_qkv) + bias_qkv + dot(low_qkv, qkv_up)).astype(bf16)
    mixed = mixed.reshape(TOK, t_count, 3, heads_here, HD)
    queries, keys, values = (
        mixed[:, :, i].reshape(TOK, heads, HD).transpose(1, 0, 2) for i in range(3)
    )
    scores = SCALE * jnp.einsum("hqd,hkd->hqk", queries, keys, preferred_element_type=f32) + additive
    probs = jax.nn.softmax(scores, axis=-1)
    probs_low = probs.astype(bf16)
    attended = jnp.einsum("hqk,hkd->hqd", probs_low, values, preferred_element_type=f32)
    attended = attended.astype(bf16).transpose(1, 0, 2).reshape(TOK, C)
    low_proj = dot(attended, proj_down).astype(bf16)
    residual = inputs + valid * (
        dot_t(attended, full_proj) + b_proj.astype(f32) + dot(low_proj, proj_up)
    )
    unit2, scale2 = norm_parts(residual)
    normed2 = (unit2 * gains[1] + shifts[1]).astype(bf16)
    low_fc1 = dot(normed2, fc1_down).astype(bf16)
    preact = dot(normed2, full_fc1) + bias_fc1 + dot(low_fc1, fc1_up)
    cdf = 0.5 * (1.0 + lax.erf(preact * (0.5**0.5)))
    hidden = (preact * cdf).astype(bf16)
    slope = cdf + preact * jnp.exp(-0.5 * preact * preact) * (0.5 / jnp.pi) ** 0.5
    low_fc2 = dot(hidden, fc2_down).astype(bf16)
    output = residual + valid * (
        dot_t(hidden, full_fc2) + b_fc2.astype(f32) + dot(low_fc2, fc2_up)
    )

    grad_branch = (valid * grad_output).astype(bf16)
    grad_fc2_up = tdot(low_fc2, grad_branch)
    grad_low_fc2 = dot_t(grad_branch, fc2_up).astype(bf16)
    grad_fc2_down = tdot(hidden, grad_low_fc2)
    grad_hidden = dot(grad_branch, full_fc2) + dot_t(grad_low_fc2, fc2_down)
    grad_preact = (grad_hidden * slope).astype(bf16)
    grad_fc1_up = tdot(low_fc1, grad_preact)
    grad_low_fc1 = dot_t(grad_preact, fc1_up).astype(bf16)
    grad_normed2 = dot_t(grad_preact, full_fc1) + dot_t(grad_low_fc1, fc1_down)
    grad_fc1_down = tdot(normed2, grad_low_fc1)
    grad_residual = grad_output + norm_back(grad_normed2, gains[1], unit2, scale2)
    grad_attn = (valid * grad_residual).astype(bf16)
    grad_proj_up = tdot(low_proj, grad_attn)
    grad_low_proj = dot_t(grad_attn, proj_up).astype(bf16)
    grad_proj_down = tdot(attended, grad_low_proj)
    grad_attended = dot(grad_attn, full_proj) + dot_t(grad_low_proj, proj_down)
    grad_attended = grad_attended.astype(bf16).reshape(TOK, heads, HD).transpose(1, 0, 2)
    grad_probs = jnp.einsum("hqd,hkd->hqk", grad_attended, values, preferred_element_type=f32)
    centre = jnp.sum(grad_probs * probs, -1, keepdims=True)
    grad_scores = (probs * (grad_probs - centre)).astype(bf16)
    grad_queries = SCALE * jnp.einsum("hqk,hkd->hqd", grad_scores, keys, preferred_element_type=f32)
    grad_keys = SCALE * jnp.einsum("hqk,hqd->hkd", grad_scores, queries, preferred_element_type=f32)
    grad_values = jnp.einsum("hqk,hqd->hkd", probs_low, grad_attended, preferred_element_type=f32)
    grad_mixed = jnp.stack([grad_queries, grad_keys, grad_values]).astype(bf16)
    grad_mixed = grad_mixed.reshape(3, t_count, heads_here, TOK, HD).transpose(3, 1, 0, 2, 4)
    grad_mixed = grad_mixed.reshape(TOK, 3 * C)
    grad_qkv_up = tdot(low_qkv, grad_mixed)
    grad_low_qkv = dot_t(grad_mixed, qkv_up).astype(bf16)
    grad_shifted = dot_t(grad_mixed, full_qkv) + dot_t(grad_low_qkv, qkv_down)
    grad_qkv_down = tdot(shifted, grad_low_qkv)
    grad_tokens = grad_residual + norm_back(grad_shifted, gains[0], unit1, scale1)

    def placed(field):
        field = field.astype(bf16).reshape(2, SHIFT, WIN, C)
        lower = swap_ctx(field[1])
        here = lax.all_gather(jnp.concatenate([lower, field[0]], 0), "tp")
        here = here.reshape(images, across, height, WIN, C).transpose(0, 2, 1, 3, 4)
        return jnp.roll(here.reshape(images, height, breadth, C), SHIFT, 2)

    output = placed(output)
    grad_tokens = placed(grad_tokens).astype(f32)

    count = 2 * z_count * t_count
    grad_main = jnp.stack([grad_qkv_down, grad_proj_down, grad_fc1_down])
    grad_main = grad_main.reshape(3, count, -1).transpose(1, 0, 2).reshape(count, -1)
    grad_out = jnp.stack([grad_proj_up, grad_fc2_up])
    grad_out = grad_out.reshape(2, count, -1).transpose(1, 0, 2).reshape(count, -1)
    grad_qkv_up = grad_qkv_up.reshape(RANK, t_count, 3, wide).transpose(0, 2, 1, 3)
    terms = [
        grad_main,
        grad_fc2_down.reshape(count, -1),
        grad_qkv_up.reshape(count, -1),
        grad_fc1_up.reshape(count, -1),
        grad_out,
    ]
    sizes = [v.shape[1] for v in terms]
    cuts = [sum(sizes[:i]) for i in range(6)]
    terms = jnp.concatenate(terms, 1).astype(bf16)
    terms = lax.all_to_all(terms, ("img", "ctx", "tp"), 0, 0, tiled=True)
    source = jnp.broadcast_to(ids[:, None, :, None], (z_count, 2, images, across)).reshape(-1)
    pick = (jnp.arange(ADAPT)[:, None] == source[None, :]).astype(bf16)
    sums = dot(pick, terms)
    grad_main, grad_fc2, grad_qkv, grad_fc1, grad_out = (
        sums[:, cuts[i] : cuts[i + 1]] for i in range(5)
    )
    return (
        output,
        grad_tokens,
        grad_main.reshape(ADAPT, 3, -1),
        grad_fc2,
        grad_qkv,
        grad_fc1,
        grad_out.reshape(ADAPT, 2, -1),
    )


def solution(mesh):
    in_specs = (
        P("img", "ctx", None, None),
        P("img", "ctx", None, None),
        P("img"),
        P("img"),
        P("ctx", None),
        P("img", None, "tp"),
        P(None, "tp"),
        P(None, "tp"),
        P("tp", "img"),
        P(),
        P("img", "tp"),
        P("tp"),
        P("tp", "img"),
        P(),
        P(),
        P(),
        P(None, None, ("img", "ctx")),
        P(None, ("img", "ctx")),
        P(None, ("img", "ctx")),
        P(None, ("img", "ctx")),
        P(None, None, ("img", "ctx")),
    )
    out_specs = (
        P("img", "ctx", None, None),
        P("img", "ctx", None, None),
        P(None, None, ("img", "ctx", "tp")),
        P(None, ("img", "ctx", "tp")),
        P(None, ("img", "ctx", "tp")),
        P(None, ("img", "ctx", "tp")),
        P(None, None, ("img", "ctx", "tp")),
    )
    return jax.shard_map(
        per_device, mesh=mesh, in_specs=in_specs, out_specs=out_specs, check_vma=False
    )
```

time: 961 us -> 747 us (0.78)
  waiting for transfers between devices: 487 us -> 12.3 us
  local copies, waits for them, and re-layouts: 135 us -> 527 us
  blocking collectives: 210 us -> 55.2 us
  starting transfers between devices: 1.28 us -> 57.9 us
  matrix products: 70.3 us -> 55.5 us
  between operations: 17.1 us -> 4.9 us
  other arithmetic: 32.4 us -> 21.7 us
    reduce_scatter x5 -> x0, waiting for transfers between devices: 407 us -> none  [the longest x1 103 us: per_device(): lax.psum_scatter(sum_fc1, ('img', 'ctx', 'tp'), scatter_dimension=1, tile...]
    dynamic_update_slice x2 -> x96, local copies, waits for them, and re-layouts: 1.07 us -> 360 us  [the longest x48 181 us: assemble(): whole = lax.dynamic_update_slice(whole, other, (top + (1 - c) * rows, left))]
    all_gather x7 -> x2, blocking collectives: 127 us -> 29.4 us  [placed(): here = lax.all_gather(jnp.concatenate([lower, field[0]], 0), 'tp')]
    psum x4 -> x0, blocking collectives: 82.7 us -> none  [the longest x1 22.2 us: per_device(): lax.psum((contract('irjtd,ctd->irjc', grad_mixed, w_qkv), contract('irjtd...]
    psum x4 -> x0, waiting for transfers between devices: 76.7 us -> none  [the longest x1 43 us: per_device(): lax.psum((contract('irjf,cf->irjc', grad_preact, w_fc1), contract('irjf,i...]
    ppermute x4 -> x83, starting transfers between devices: 0.6 us -> 49.1 us  [the longest x9 14.5 us: ring(): lax.ppermute(held[-1], 'img', [(i, (i + 1) % count) for i in range(count)])]
    squeeze x0 -> x46, local copies, waits for them, and re-layouts: none -> 44.2 us  [the longest x24 22.7 us: spread_last(): out[k, two], out[k, one + two] = (other[0], other[1])]
    gather x1 -> x0, local copies, waits for them, and re-layouts: 39 us -> none  [per_device(): rel_table.astype(jnp.float32)[relative_index()]]
  transfers between devices with their start and end apart: 15 -> 85, of which waited for: 8 -> 5; matrix products, arithmetic and copies ran while one was open for 15% -> 74% of each run, Pallas kernels for 0% -> 0%
where the time goes in v1:
time: 747 us; the launch traced here: 734 us
  local copies, waits for them, and re-layouts  527 us (71%)
  starting transfers between devices  57.9 us (8%)
  matrix products  55.5 us (7%)
  blocking collectives  55.2 us (7%)
  other arithmetic  21.7 us (3%)
  waiting for transfers between devices  12.3 us (2%)
    dynamic_update_slice x48, local copies, waits for them, and re-layouts, assemble(): whole = lax.dynamic_update_slice(whole, other, (top + (1 - c) * rows, left))  181 us
    dynamic_update_slice x48, local copies, waits for them, and re-layouts, assemble(): whole = lax.dynamic_update_slice(whole, piece, (top + c * rows, left))  179 us
    ppermute x32, local copies, waits for them, and re-layouts, swap_ctx(): return lax.ppermute(v, 'ctx', [(0, 1), (1, 0)])  37.2 us
    all_gather x2, blocking collectives, placed(): here = lax.all_gather(jnp.concatenate([lower, field[0]], 0), 'tp')  29.4 us
    unnamed x256, local copies, waits for them, and re-layouts  27.2 us
    unnamed x2, blocking collectives  25.7 us
    squeeze x24, local copies, waits for them, and re-layouts, spread_last(): out[k, two], out[k, one + two] = (other[0], other[1])  22.7 us
    dot_general x15, matrix products, dot(): return jnp.dot(left, right, preferred_element_type=f32)  21.7 us
  transfers between devices with their start and end apart: 85, of which 5 were waited for; matrix products, arithmetic and copies ran while one was open for 74% of the time, Pallas kernels for 0%

profile of v1, /device:TPU:0, one launch (start us, length us, event | category | flops | bytes accessed | tf_op | source)
XLA Modules:
  0.0 734.5 jit_solution(6859794441186418990)
XLA Ops:
  9.3 8.7 %all-reduce.1 = s32[8]{0:T(128)S(1)} all-reduce(s32[8]{0:T(128)S(1)} %dynamic-update-slice.1), channel_id=3, replica_groups=mesh['img'=4,'ctx'=2,'tp'=4] {'img'}, use_global_device_ids=true, to_apply=%add.1 | all-reduce | flops 8 | bytes 64
  31.3 17.0 %all-reduce = bf16[18072]{0:T(1024)(128)(2,1)S(1)} all-reduce(bf16[18072]{0:T(1024)(128)(2,1)S(1)} %dynamic-update-slice), channel_id=2, replica_groups=mesh['img'=4,'ctx'=2,'tp'=4] {'tp'}, use_global_device_ids=true, to_apply=%add | all-reduce | flops 18072 | bytes 72288
  72.1 5.6 copy.326
  114.6 4.0 dynamic_update_slice.354
  197.4 4.0 dynamic_update_slice.298
  205.3 4.0 dynamic_update_slice.300
  216.1 4.1 dynamic_update_slice.302
  244.6 4.0 dynamic_update_slice.325
  253.9 4.0 dynamic_update_slice.327
  257.9 4.0 dynamic_update_slice.328
  317.5 4.0 dynamic_update_slice.307
  384.5 4.0 dynamic_update_slice.315
  420.5 4.0 convolution_convert_fusion.3
  480.2 4.1 dynamic_update_slice.369
  500.1 5.0 collective-permute-done.54
  529.0 4.1 dynamic_update_slice.341
  542.2 4.0 dynamic_update_slice.344
  548.0 4.0 dynamic_update_slice.345
  588.0 4.1 dynamic_update_slice.379
  631.6 4.7 multiply_convert_fusion.1
  654.2 4.9 convolution_convert_fusion.4
  679.3 5.4 all-to-all-start.1
  692.2 15.8 %all-gather.3 = bf16[48,12,768]{2,1,0:T(8,128)(2,1)S(1)} all-gather(bf16[12,12,768]{2,1,0:T(8,128)(2,1)S(1)} %pad_maximum_fusion.6), channel_id=5, replica_groups=mesh['img'=4,'ctx'=2,'tp'=4] {'tp'}, dimensions={0}, use_global_device_ids=true | all-gather | bytes 1105920 | tf_op jit(solution)/shard_map/all_gather | solution.py:273
  709.7 13.6 %all-gather.2 = bf16[48,12,768]{2,1,0:T(8,128)(2,1)S(1)} all-gather(bf16[12,12,768]{2,1,0:T(8,128)(2,1)S(1)} %pad_maximum_fusion.5), channel_id=4, replica_groups=mesh['img'=4,'ctx'=2,'tp'=4] {'tp'}, dimensions={0}, use_global_device_ids=true | all-gather | bytes 1105920 | tf_op jit(solution)/shard_map/all_gather | solution.py:273
  (760 shorter events, 588.0 us)
Async XLA Ops:
  2.9 115.6 %collective-permute-start.1 = (bf16[96,768]{0,1:T(8,128)(2,1)S(1)}, bf16[96,768]{0,1:T(8,128)(2,1)}, u32[]{:S(2)}, u32[]{:S(2)}) collective-permute-start(bf16[96,768]{0,1:T(8,128)(2,1)S(1)} %pad_maximum_fusion.7), channel_id=1, source_target_pairs={{0,4},{4,0},{1,5},{5,1},{2,6},{6,2},{3,7},{7,3},{8,12},{12,8},{9,1... | collective-permute-start | bytes 442376 | tf_op jit(solution)/shard_map/ppermute | solution.py:35
  3.5 116.3 %collective-permute-start.2 = (bf16[96,768]{0,1:T(8,128)(2,1)S(1)}, bf16[96,768]{0,1:T(8,128)(2,1)}, u32[]{:S(2)}, u32[]{:S(2)}) collective-permute-start(bf16[96,768]{0,1:T(8,128)(2,1)S(1)} %pad_maximum_fusion.7), channel_id=1, source_target_pairs={{0,1},{1,0},{2,3},{3,2},{4,5},{5,4},{6,7},{7,6},{8,9},{9,8},{10,11... | collective-permute-start | bytes 442376 | tf_op jit(solution)/shard_map/ppermute | solution.py:39
  6.0 61.6 %collective-permute-start.33 = (bf16[96,768]{1,0:T(8,128)(2,1)S(1)}, bf16[96,768]{1,0:T(8,128)(2,1)}, u32[]{:S(2)}, u32[]{:S(2)}) collective-permute-start(bf16[96,768]{1,0:T(8,128)(2,1)S(1)} %constant_dynamic-slice_fusion), channel_id=1, source_target_pairs={{0,4},{4,0},{1,5},{5,1},{2,6},{6,2},{3,7},{7,3},{8,12},{12,8},{9,1... | collective-permute-start | bytes 442376 | tf_op jit(solution)/shard_map/ppermute | solution.py:35
  6.3 103.1 %collective-permute-start.34 = (bf16[96,768]{1,0:T(8,128)(2,1)S(1)}, bf16[96,768]{1,0:T(8,128)(2,1)S(1)}, u32[]{:S(2)}, u32[]{:S(2)}) collective-permute-start(bf16[96,768]{1,0:T(8,128)(2,1)S(1)} %constant_dynamic-slice_fusion), channel_id=1, source_target_pairs={{0,1},{1,0},{2,3},{3,2},{4,5},{5,4},{6,7},{7,6},{8,9},{9,8},{10,11... | collective-permute-start | bytes 442376 | tf_op jit(solution)/shard_map/ppermute | solution.py:39
  25.3 110.7 %all-to-all-start = ((bf16[4,2,12288]{2,1,0:T(2,128)(2,1)}), bf16[4,2,12288]{2,1,0:T(2,128)(2,1)S(1)}, u32[]{:S(2)}, u32[]{:S(2)}) async-start(bf16[4,2,12288]{2,1,0:T(2,128)(2,1)} %reshape.525), calls=%async_computation | async-start | bytes 393216 | tf_op jit(solution)/shard_map/all_to_all | solution.py:181
  29.4 73.7 %collective-permute-start.57 = (bf16[96,768]{1,0:T(8,128)(2,1)}, bf16[96,768]{1,0:T(8,128)(2,1)}, u32[]{:S(2)}, u32[]{:S(2)}) collective-permute-start(bf16[96,768]{1,0:T(8,128)(2,1)} %get-tuple-element.82), channel_id=1, source_target_pairs={{0,4},{4,0},{1,5},{5,1},{2,6},{6,2},{3,7},{7,3},{8,12},{12,8},{9,1... | collective-permute-start | bytes 442376 | tf_op jit(solution)/shard_map/ppermute | solution.py:35
  113.8 49.9 %collective-permute-start.36 = (bf16[2,96,768]{2,1,0:T(8,128)(2,1)}, bf16[2,96,768]{2,1,0:T(8,128)(2,1)}, u32[]{:S(2)}, u32[]{:S(2)}) collective-permute-start(bf16[2,96,768]{2,1,0:T(8,128)(2,1)} %pad_maximum_fusion.3), channel_id=1, source_target_pairs={{0,2},{2,0},{1,3},{3,1},{4,6},{6,4},{5,7},{7,5},{8,10},{10,8},{9,1... | collective-permute-start | bytes 884744 | tf_op jit(solution)/shard_map/ppermute | solution.py:43
  230.7 103.5 %collective-permute-start.42 = (bf16[2,96,768]{2,1,0:T(8,128)(2,1)}, bf16[2,96,768]{2,1,0:T(8,128)(2,1)}, u32[]{:S(2)}, u32[]{:S(2)}) collective-permute-start(bf16[2,96,768]{2,1,0:T(8,128)(2,1)} %collective-permute-done.39), channel_id=1, source_target_pairs={{0,2},{2,0},{1,3},{3,1},{4,6},{6,4},{5,7},{7,5},{8,10},{10,8},{9,1... | collective-permute-start | bytes 884744 | tf_op jit(solution)/shard_map/ppermute | solution.py:43
  233.8 91.3 %collective-permute-start.21 = (bf16[96,768]{0,1:T(8,128)(2,1)}, bf16[96,768]{0,1:T(8,128)(2,1)}, u32[]{:S(2)}, u32[]{:S(2)}) collective-permute-start(bf16[96,768]{0,1:T(8,128)(2,1)} %collective-permute-done.20), channel_id=1, source_target_pairs={{0,4},{4,0},{1,5},{5,1},{2,6},{6,2},{3,7},{7,3},{8,12},{12,8},{9,1... | collective-permute-start | bytes 442376 | tf_op jit(solution)/shard_map/ppermute | solution.py:35
  234.0 95.3 %collective-permute-start.22 = (bf16[96,768]{0,1:T(8,128)(2,1)}, bf16[96,768]{0,1:T(8,128)(2,1)}, u32[]{:S(2)}, u32[]{:S(2)}) collective-permute-start(bf16[96,768]{0,1:T(8,128)(2,1)} %collective-permute-done.20), channel_id=1, source_target_pairs={{0,1},{1,0},{2,3},{3,2},{4,5},{5,4},{6,7},{7,6},{8,9},{9,8},{10,11... | collective-permute-start | bytes 442376 | tf_op jit(solution)/shard_map/ppermute | solution.py:39
  235.5 102.5 %collective-permute-start.45 = (bf16[2,96,768]{2,1,0:T(8,128)(2,1)}, bf16[2,96,768]{2,1,0:T(8,128)(2,1)}, u32[]{:S(2)}, u32[]{:S(2)}) collective-permute-start(bf16[2,96,768]{2,1,0:T(8,128)(2,1)} %collective-permute-done.39), channel_id=1, source_target_pairs={{0,8},{8,16},{16,24},{24,0},{1,9},{9,17},{17,25},{25,1},{2,10},{10... | collective-permute-start | bytes 884744 | tf_op jit(solution)/shard_map/ppermute | solution.py:54
  238.2 78.6 %collective-permute-start.19 = (bf16[96,768]{0,1:T(8,128)(2,1)}, bf16[96,768]{0,1:T(8,128)(2,1)}, u32[]{:S(2)}, u32[]{:S(2)}) collective-permute-start(bf16[96,768]{0,1:T(8,128)(2,1)} %collective-permute-done.18), channel_id=1, source_target_pairs={{0,4},{4,0},{1,5},{5,1},{2,6},{6,2},{3,7},{7,3},{8,12},{12,8},{9,1... | collective-permute-start | bytes 442376 | tf_op jit(solution)/shard_map/ppermute | solution.py:35
  316.8 59.3 %collective-permute-start.25 = (bf16[96,768]{0,1:T(8,128)(2,1)}, bf16[96,768]{0,1:T(8,128)(2,1)S(1)}, u32[]{:S(2)}, u32[]{:S(2)}) collective-permute-start(bf16[96,768]{0,1:T(8,128)(2,1)} %collective-permute-done.24), channel_id=1, source_target_pairs={{0,4},{4,0},{1,5},{5,1},{2,6},{6,2},{3,7},{7,3},{8,12},{12,8},{9,1... | collective-permute-start | bytes 442376 | tf_op jit(solution)/shard_map/ppermute | solution.py:35
  368.2 57.9 %collective-permute-start.43 = (bf16[96,768]{1,0:T(8,128)(2,1)}, bf16[96,768]{1,0:T(8,128)(2,1)}, u32[]{:S(2)}, u32[]{:S(2)}) collective-permute-start(bf16[96,768]{1,0:T(8,128)(2,1)} %get-tuple-element.92), channel_id=1, source_target_pairs={{0,4},{4,0},{1,5},{5,1},{2,6},{6,2},{3,7},{7,3},{8,12},{12,8},{9,1... | collective-permute-start | bytes 442376 | tf_op jit(solution)/shard_map/ppermute | solution.py:35
  376.1 50.9 %collective-permute-start.44 = (bf16[96,768]{1,0:T(8,128)(2,1)}, bf16[96,768]{1,0:T(8,128)(2,1)}, u32[]{:S(2)}, u32[]{:S(2)}) collective-permute-start(bf16[96,768]{1,0:T(8,128)(2,1)} %get-tuple-element.91), channel_id=1, source_target_pairs={{0,4},{4,0},{1,5},{5,1},{2,6},{6,2},{3,7},{7,3},{8,12},{12,8},{9,1... | collective-permute-start | bytes 442376 | tf_op jit(solution)/shard_map/ppermute | solution.py:35
  426.1 66.7 %collective-permute-start.48 = (bf16[2,96,768]{2,1,0:T(8,128)(2,1)}, bf16[2,96,768]{2,1,0:T(8,128)(2,1)}, u32[]{:S(2)}, u32[]{:S(2)}) collective-permute-start(bf16[2,96,768]{2,1,0:T(8,128)(2,1)} %collective-permute-done.45), channel_id=1, source_target_pairs={{0,2},{2,0},{1,3},{3,1},{4,6},{6,4},{5,7},{7,5},{8,10},{10,8},{9,1... | collective-permute-start | bytes 884744 | tf_op jit(solution)/shard_map/ppermute | solution.py:43
  427.6 60.2 %collective-permute-start.71 = (bf16[96,768]{1,0:T(8,128)(2,1)}, bf16[96,768]{1,0:T(8,128)(2,1)}, u32[]{:S(2)}, u32[]{:S(2)}) collective-permute-start(bf16[96,768]{1,0:T(8,128)(2,1)} %get-tuple-element.73), channel_id=1, source_target_pairs={{0,4},{4,0},{1,5},{5,1},{2,6},{6,2},{3,7},{7,3},{8,12},{12,8},{9,1... | collective-permute-start | bytes 442376 | tf_op jit(solution)/shard_map/ppermute | solution.py:35
  427.7 66.6 %collective-permute-start.51 = (bf16[2,96,768]{2,1,0:T(8,128)(2,1)}, bf16[2,96,768]{2,1,0:T(8,128)(2,1)}, u32[]{:S(2)}, u32[]{:S(2)}) collective-permute-start(bf16[2,96,768]{2,1,0:T(8,128)(2,1)} %collective-permute-done.45), channel_id=1, source_target_pairs={{0,8},{8,16},{16,24},{24,0},{1,9},{9,17},{17,25},{25,1},{2,10},{10... | collective-permute-start | bytes 884744 | tf_op jit(solution)/shard_map/ppermute | solution.py:54
  507.8 79.2 %collective-permute-start.77 = (bf16[96,768]{1,0:T(8,128)(2,1)}, bf16[96,768]{1,0:T(8,128)(2,1)}, u32[]{:S(2)}, u32[]{:S(2)}) collective-permute-start(bf16[96,768]{1,0:T(8,128)(2,1)} %get-tuple-element.69), channel_id=1, source_target_pairs={{0,4},{4,0},{1,5},{5,1},{2,6},{6,2},{3,7},{7,3},{8,12},{12,8},{9,1... | collective-permute-start | bytes 442376 | tf_op jit(solution)/shard_map/ppermute | solution.py:35
  508.3 95.9 %collective-permute-start.55 = (bf16[96,768]{1,0:T(8,128)(2,1)}, bf16[96,768]{1,0:T(8,128)(2,1)}, u32[]{:S(2)}, u32[]{:S(2)}) collective-permute-start(bf16[96,768]{1,0:T(8,128)(2,1)} %get-tuple-element.84), channel_id=1, source_target_pairs={{0,4},{4,0},{1,5},{5,1},{2,6},{6,2},{3,7},{7,3},{8,12},{12,8},{9,1... | collective-permute-start | bytes 442376 | tf_op jit(solution)/shard_map/ppermute | solution.py:35
  508.4 104.6 %collective-permute-start.56 = (bf16[96,768]{1,0:T(8,128)(2,1)}, bf16[96,768]{1,0:T(8,128)(2,1)}, u32[]{:S(2)}, u32[]{:S(2)}) collective-permute-start(bf16[96,768]{1,0:T(8,128)(2,1)} %get-tuple-element.83), channel_id=1, source_target_pairs={{0,4},{4,0},{1,5},{5,1},{2,6},{6,2},{3,7},{7,3},{8,12},{12,8},{9,1... | collective-permute-start | bytes 442376 | tf_op jit(solution)/shard_map/ppermute | solution.py:35
  508.8 109.1 %collective-permute-start.79 = (bf16[96,768]{1,0:T(8,128)(2,1)}, bf16[96,768]{1,0:T(8,128)(2,1)}, u32[]{:S(2)}, u32[]{:S(2)}) collective-permute-start(bf16[96,768]{1,0:T(8,128)(2,1)} %get-tuple-element.68), channel_id=1, source_target_pairs={{0,4},{4,0},{1,5},{5,1},{2,6},{6,2},{3,7},{7,3},{8,12},{12,8},{9,1... | collective-permute-start | bytes 442376 | tf_op jit(solution)/shard_map/ppermute | solution.py:35
  509.6 117.2 %collective-permute-start.80 = (bf16[96,768]{1,0:T(8,128)(2,1)}, bf16[96,768]{1,0:T(8,128)(2,1)}, u32[]{:S(2)}, u32[]{:S(2)}) collective-permute-start(bf16[96,768]{1,0:T(8,128)(2,1)} %get-tuple-element.67), channel_id=1, source_target_pairs={{0,4},{4,0},{1,5},{5,1},{2,6},{6,2},{3,7},{7,3},{8,12},{12,8},{9,1... | collective-permute-start | bytes 442376 | tf_op jit(solution)/shard_map/ppermute | solution.py:35
  679.3 50.0 %all-to-all-start.1 = ((bf16[32,2,3072]{2,1,0:T(2,128)(2,1)}), bf16[32,2,3072]{2,1,0:T(2,128)(2,1)}, u32[]{:S(2)}, u32[]{:S(2)}) async-start(bf16[32,2,3072]{2,1,0:T(2,128)(2,1)} %reshape.527), calls=%async_computation.1 | async-start | bytes 786432 | tf_op jit(solution)/shard_map/all_to_all | solution.py:296
  (172 other events, 2710.6 us)
